TPU v7x, 512 devices: a whole 4x4x16 slice. The times are simulated.
512 devices in a mesh: tm: 32 (over x, y, core), tile: 16 (over z).
Axes of the slice: x: 4, y: 4, z: 16, core: 2. Of those that a mesh axis runs over, the one named last changes fastest.
Arguments:
- seg_gain: bfloat16 [32, 1024, 1024], P('tm', 'tile'), may hold values from -0.1875 to 0.1875
- seg_offset: float32 [32, 1024], P('tm', 'tile'), may hold values from -6 to 6
- seg_noise: bfloat16 [32, 1024, 1024], P('tm', 'tile'), as said below
- end_mean: bfloat16 [8, 1024], P(None, 'tile'), may hold values from -6 to 6
- end_cov: bfloat16 [8, 1024, 1024], P(None, 'tile'), as said below
- step_gain: bfloat16 [256, 1024, 1024], P('tm', 'tile'), may hold values from -0.1875 to 0.1875
- step_offset: float32 [256, 1024], P('tm', 'tile'), may hold values from -6 to 6
- step_var: float32 [256, 1024], P('tm', 'tile'), may hold values from 0.1 to 1.5
- obs_tiles: int32 [256, 4], P('tm'), may hold values from 0 to 7
- obs_count: int32 [256], P('tm'), may hold values from 1 to 4, as said below
- obs_value: float32 [256, 4, 128], P('tm'), may hold values from -10 to 10
- obs_noise: float32 [1024], replicated, may hold values from 0.2 to 2
Outputs:
- start_cov: bfloat16 [32, 1024, 1024], P('tm', 'tile')
- start_mean: bfloat16 [32, 1024], P('tm', 'tile')
- step_mean: float32 [256, 1024], P('tm', 'tile')
- step_spread: float32 [256, 1024], P('tm', 'tile')
- innovation: float32 [256, 4, 128], P('tm')
Inputs may be any that keep to these rules, and one draw needn't show every extreme that they name: `end_cov`: each matrix is symmetric and positive definite. `seg_noise`: each matrix is symmetric and positive definite. `obs_count`: some step has 4 live slots and some has 1.
All inputs are finite; a program needn't handle non-finite values.
Results may differ from a plain program's by a relative error of at most 0.015.
Values may be sent and summed in bfloat16 or wider, within the bound.
A program may use at most 64 MiB of HBM per device.

v0:
```python
import jax
import jax.numpy as jnp
from jax import lax
from jax.sharding import PartitionSpec as P

TILE_STATES = 128
SLOTS = 4
GROUP_SEGS = 4


def shifted(block, axis, distance):
    devices = range(lax.axis_size(axis))
    route = [(i - distance, i) for i in devices if i - distance in devices]
    return lax.ppermute(block, axis, route)


def shards(
    seg_gain,
    seg_offset,
    seg_noise,
    end_mean,
    end_cov,
    step_gain,
    step_offset,
    step_var,
    obs_tiles,
    obs_count,
    obs_value,
    obs_noise,
):
    position = lax.axis_index("tm")
    slot_place = position % GROUP_SEGS
    group_index = position // GROUP_SEGS
    gain_rows = seg_gain[0]
    offset_rows = seg_offset[0]
    noise_rows = seg_noise[0].astype(jnp.float32)
    row_count = gain_rows.shape[0]
    state_count = gain_rows.shape[1]
    cur_mean = lax.dynamic_index_in_dim(end_mean, group_index, 0, keepdims=False)
    cur_cov = lax.dynamic_index_in_dim(end_cov, group_index, 0, keepdims=False)
    kept_mean = jnp.zeros((state_count,), jnp.bfloat16)
    kept_cov = jnp.zeros((state_count, state_count), jnp.bfloat16)
    out_mean = jnp.zeros((row_count,), jnp.bfloat16)
    out_cov = jnp.zeros((row_count, state_count), jnp.bfloat16)
    for depth_step in range(GROUP_SEGS):
        whole_mean, whole_cov = (
            lax.all_gather(cur_mean, "tile", axis=0, tiled=True),
            lax.all_gather(cur_cov, "tile", axis=0, tiled=True),
        )
        is_mine = slot_place == GROUP_SEGS - 1 - depth_step
        kept_mean = jnp.where(is_mine, whole_mean, kept_mean)
        kept_cov = jnp.where(is_mine, whole_cov, kept_cov)
        product = jnp.dot(gain_rows, whole_cov, preferred_element_type=jnp.float32).astype(
            jnp.bfloat16
        )
        col_block = jnp.einsum(
            "pd,rd->pr",
            lax.all_gather(product, "tile", axis=0, tiled=True),
            gain_rows,
            preferred_element_type=jnp.float32,
        )
        spread_rows = lax.all_to_all(col_block, "tile", split_axis=0, concat_axis=1, tiled=True)
        new_cov = (spread_rows + noise_rows).astype(jnp.bfloat16)
        new_mean = (
            jnp.dot(gain_rows, whole_mean, preferred_element_type=jnp.float32) + offset_rows
        ).astype(jnp.bfloat16)
        out_mean = jnp.where(is_mine, new_mean, out_mean)
        out_cov = jnp.where(is_mine, new_cov, out_cov)
        if depth_step < GROUP_SEGS - 1:
            got_mean, got_cov = shifted((new_mean, new_cov), "tm", -1)
            takes_next = slot_place == GROUP_SEGS - 2 - depth_step
            cur_mean = jnp.where(takes_next, got_mean, cur_mean)
            cur_cov = jnp.where(takes_next, got_cov, cur_cov)
    partial_value = jnp.einsum(
        "krd,de->kre", step_gain, kept_cov, preferred_element_type=jnp.float32
    )
    local_spread = jnp.sum(partial_value * step_gain, axis=2) + step_var
    local_mean = (
        jnp.einsum("krd,d->kr", step_gain, kept_mean, preferred_element_type=jnp.float32)
        + step_offset
    )
    full_mean, full_spread = (
        lax.all_gather(local_mean, "tile", axis=1, tiled=True),
        lax.all_gather(local_spread, "tile", axis=1, tiled=True),
    )
    step_count = full_mean.shape[0]
    tile_total = state_count // TILE_STATES
    tile_mean = full_mean.reshape(step_count, tile_total, TILE_STATES)
    tile_spread = full_spread.reshape(step_count, tile_total, TILE_STATES) + obs_noise.reshape(
        1, tile_total, TILE_STATES
    )
    onehot = (
        obs_tiles[:, :, None] == jnp.arange(tile_total, dtype=jnp.int32)[None, None, :]
    ).astype(jnp.float32)
    picked_mean = jnp.einsum("ksn,kno->kso", onehot, tile_mean, precision=lax.Precision.HIGHEST)
    picked_spread = jnp.einsum("ksn,kno->kso", onehot, tile_spread, precision=lax.Precision.HIGHEST)
    live_slots = jnp.arange(SLOTS, dtype=jnp.int32)[None, :] < obs_count[:, None]
    innovation = jnp.where(
        live_slots[:, :, None], (obs_value - picked_mean) / picked_spread, jnp.float32(0.0)
    )
    return (out_cov[None], out_mean[None], local_mean, local_spread, innovation)


def solution(mesh):
    in_specs = (
        P("tm", "tile", None),
        P("tm", "tile"),
        P("tm", "tile", None),
        P(None, "tile"),
        P(None, "tile", None),
        P("tm", "tile", None),
        P("tm", "tile"),
        P("tm", "tile"),
        P("tm", None),
        P("tm"),
        P("tm", None, None),
        P(),
    )
    out_specs = (
        P("tm", "tile", None),
        P("tm", "tile"),
        P("tm", "tile"),
        P("tm", "tile"),
        P("tm", None, None),
    )
    return jax.shard_map(shards, mesh=mesh, in_specs=in_specs, out_specs=out_specs, check_vma=False)
```

profile of v0, /device:TPU:2, one launch (start us, length us, event | category | flops | bytes accessed | tf_op | source)
XLA Modules:
  0.0 827.4 jit_solution(18395162919575817385)
XLA Ops:
  8.9 79.4 %all-gather.27.cloned.1.call-done = bf16[1,1024,1024]{2,1,0:T(8,128)(2,1)} async-done(((bf16[1,64,1024]{2,1,0:T(8,128)(2,1)}), bf16[1,1024,1024]{2,1,0:T(8,128)(2,1)}) %all-gather.27.cloned.1.call-update) | async-done | bytes 2097168 | tf_op jit(solution)/shard_map/all_gather | solution.py:48
  88.3 2.7 fusion.19
  91.1 70.2 %all-gather.13.cloned.1.call-done = bf16[1024,1024]{1,0:T(8,128)(2,1)} async-done(((bf16[64,1024]{1,0:T(8,128)(2,1)}), bf16[1024,1024]{1,0:T(8,128)(2,1)}) %all-gather.13.cloned.1.call-update) | async-done | bytes 2097168 | tf_op jit(solution)/shard_map/all_gather | solution.py:58
  163.9 21.7 %all_to_all.73 = f32[16,1,4096]{2,1,0:T(1,128)S(1)} all-to-all(f32[16,1,4096]{2,1,0:T(1,128)S(1)} %reshape.104), channel_id=1, replica_groups=mesh['tm'=32,'tile'=16] {'tile'}, dimensions={0} | all-to-all | bytes 524288 | tf_op jit(solution)/shard_map/all_to_all | solution.py:62
  194.1 69.4 %all-gather.15.cloned.1.call-done = bf16[1024,1024]{1,0:T(8,128)(2,1)} async-done(((bf16[64,1024]{1,0:T(8,128)(2,1)}), bf16[1024,1024]{1,0:T(8,128)(2,1)}) %all-gather.15.cloned.1.call-update) | async-done | bytes 2097168 | tf_op jit(solution)/shard_map/all_gather | solution.py:48
  263.5 2.7 fusion.16
  266.3 70.3 %all-gather.17.cloned.1.call-done = bf16[1024,1024]{1,0:T(8,128)(2,1)} async-done(((bf16[64,1024]{1,0:T(8,128)(2,1)}), bf16[1024,1024]{1,0:T(8,128)(2,1)}) %all-gather.17.cloned.1.call-update) | async-done | bytes 2097168 | tf_op jit(solution)/shard_map/all_gather | solution.py:58
  339.2 21.8 %all_to_all.74 = f32[16,1,4096]{2,1,0:T(1,128)S(1)} all-to-all(f32[16,1,4096]{2,1,0:T(1,128)S(1)} %reshape.106), channel_id=1, replica_groups=mesh['tm'=32,'tile'=16] {'tile'}, dimensions={0} | all-to-all | bytes 524288 | tf_op jit(solution)/shard_map/all_to_all | solution.py:62
  364.8 2.5 collective-permute-done.1
  368.1 69.4 %all-gather.19.cloned.1.call-done = bf16[1024,1024]{1,0:T(8,128)(2,1)} async-done(((bf16[64,1024]{1,0:T(8,128)(2,1)}), bf16[1024,1024]{1,0:T(8,128)(2,1)}) %all-gather.19.cloned.1.call-update) | async-done | bytes 2097168 | tf_op jit(solution)/shard_map/all_gather | solution.py:48
  437.5 2.7 fusion.17
  440.3 70.3 %all-gather.21.cloned.1.call-done = bf16[1024,1024]{1,0:T(8,128)(2,1)} async-done(((bf16[64,1024]{1,0:T(8,128)(2,1)}), bf16[1024,1024]{1,0:T(8,128)(2,1)}) %all-gather.21.cloned.1.call-update) | async-done | bytes 2097168 | tf_op jit(solution)/shard_map/all_gather | solution.py:58
  513.2 21.8 %all_to_all.75 = f32[16,1,4096]{2,1,0:T(1,128)S(1)} all-to-all(f32[16,1,4096]{2,1,0:T(1,128)S(1)} %reshape.108), channel_id=1, replica_groups=mesh['tm'=32,'tile'=16] {'tile'}, dimensions={0} | all-to-all | bytes 524288 | tf_op jit(solution)/shard_map/all_to_all | solution.py:62
  538.9 2.5 collective-permute-done.2
  542.2 69.4 %all-gather.23.cloned.1.call-done = bf16[1024,1024]{1,0:T(8,128)(2,1)} async-done(((bf16[64,1024]{1,0:T(8,128)(2,1)}), bf16[1024,1024]{1,0:T(8,128)(2,1)}) %all-gather.23.cloned.1.call-update) | async-done | bytes 2097168 | tf_op jit(solution)/shard_map/all_gather | solution.py:48
  611.6 2.7 fusion.18
  616.6 29.9 %all-reduce = bf16[1024]{0:T(1024)(128)(2,1)S(1)} all-reduce(bf16[1024]{0:T(1024)(128)(2,1)S(1)} %dynamic-update-slice), channel_id=3, replica_groups=mesh['tm'=32,'tile'=16] {'tile'}, use_global_device_ids=true, to_apply=%add | all-reduce | flops 1024 | bytes 4096 | tf_op jit(solution)/shard_map/all_gather | solution.py:47
  650.1 27.1 %all-reduce.1 = bf16[1024]{0:T(1024)(128)(2,1)S(1)} all-reduce(bf16[1024]{0:T(1024)(128)(2,1)S(1)} %dynamic-update-slice.1), channel_id=1, replica_groups=mesh['tm'=32,'tile'=16] {'tile'}, use_global_device_ids=true, to_apply=%add.1 | all-reduce | flops 1024 | bytes 4096
  680.8 29.1 %all-reduce.2 = bf16[1024]{0:T(1024)(128)(2,1)S(1)} all-reduce(bf16[1024]{0:T(1024)(128)(2,1)S(1)} %dynamic-update-slice.2), channel_id=1, replica_groups=mesh['tm'=32,'tile'=16] {'tile'}, use_global_device_ids=true, to_apply=%add.2 | all-reduce | flops 1024 | bytes 4096
  713.4 27.2 %all-reduce.3 = bf16[1024]{0:T(1024)(128)(2,1)S(1)} all-reduce(bf16[1024]{0:T(1024)(128)(2,1)S(1)} %dynamic-update-slice.3), channel_id=1, replica_groups=mesh['tm'=32,'tile'=16] {'tile'}, use_global_device_ids=true, to_apply=%add.3 | all-reduce | flops 1024 | bytes 4096
  742.5 28.3 %all-gather.2 = f32[16,64,8]{1,2,0:T(8,128)S(1)} all-gather(f32[1,64,8]{1,2,0:T(8,128)S(1)} %bitcast.172), channel_id=1, replica_groups=mesh['tm'=32,'tile'=16] {'tile'}, dimensions={0}, use_global_device_ids=true | all-gather | bytes 34816 | tf_op jit(solution)/shard_map/all_gather | solution.py:83
  776.4 6.6 all-to-all-start.3
  783.0 3.8 fusion
  786.8 30.1 %all-gather.3 = f32[16,64,8]{1,2,0:T(8,128)S(1)} all-gather(f32[1,64,8]{1,2,0:T(8,128)S(1)} %bitcast.173), channel_id=1, replica_groups=mesh['tm'=32,'tile'=16] {'tile'}, dimensions={0}, use_global_device_ids=true | all-gather | bytes 34816 | tf_op jit(solution)/shard_map/all_gather | solution.py:84
  (130 shorter events, 50.5 us)
Async XLA Ops:
  7.2 81.1 %copy-start = (bf16[1,64,1024]{2,1,0:T(8,128)(2,1)S(1)}, bf16[1,64,1024]{2,1,0:T(8,128)(2,1)}, u32[]{:S(2)}) copy-start(bf16[1,64,1024]{2,1,0:T(8,128)(2,1)} %param.12) | copy-start | bytes 393220
  7.2 81.1 %all-gather.27.cloned.1.call-start = ((), (), s32[]{:S(2)}) async-start(), calls=%async_computation.11 | async-start | bytes 2228224 | tf_op jit(solution)/shard_map/all_gather | solution.py:48
  8.8 152.4 %all-gather.13.cloned.1.call-start = ((), (), s32[]{:S(2)}) async-start(), calls=%async_computation.4 | async-start | bytes 2228224 | tf_op jit(solution)/shard_map/all_gather | solution.py:58
  91.0 172.5 %all-gather.15.cloned.1.call-start = ((), (), s32[]{:S(2)}) async-start(), calls=%async_computation.5 | async-start | bytes 2228224 | tf_op jit(solution)/shard_map/all_gather | solution.py:48
  188.0 4.4 collective-permute-start
  194.0 142.6 %all-gather.17.cloned.1.call-start = ((), (), s32[]{:S(2)}) async-start(), calls=%async_computation.6 | async-start | bytes 2228224 | tf_op jit(solution)/shard_map/all_gather | solution.py:58
  266.2 171.3 %all-gather.19.cloned.1.call-start = ((), (), s32[]{:S(2)}) async-start(), calls=%async_computation.7 | async-start | bytes 2228224 | tf_op jit(solution)/shard_map/all_gather | solution.py:48
  362.9 4.4 collective-permute-start.1
  368.0 142.6 %all-gather.21.cloned.1.call-start = ((), (), s32[]{:S(2)}) async-start(), calls=%async_computation.8 | async-start | bytes 2228224 | tf_op jit(solution)/shard_map/all_gather | solution.py:58
  440.3 171.3 %all-gather.23.cloned.1.call-start = ((), (), s32[]{:S(2)}) async-start(), calls=%async_computation.9 | async-start | bytes 2228224 | tf_op jit(solution)/shard_map/all_gather | solution.py:48
  536.8 79.6 %copy-start.12 = (bf16[8,64]{1,0:T(8,128)(2,1)S(1)}, bf16[8,64]{1,0:T(8,128)(2,1)}, u32[]{:S(2)}) copy-start(bf16[8,64]{1,0:T(8,128)(2,1)} %param.15) | copy-start | bytes 3076
  536.8 109.8 %copy-start.15 = (f32[1,64]{1,0:T(1,128)S(1)}, f32[1,64]{1,0:T(1,128)}, u32[]{:S(2)}) copy-start(f32[1,64]{1,0:T(1,128)} %param.13) | copy-start | bytes 772
  537.0 142.3 %copy-start.14 = (s32[8]{0:T(128)S(1)}, s32[8]{0:T(128)}, u32[]{:S(2)}) copy-start(s32[8]{0:T(128)} %param.21) | copy-start | bytes 100
  537.0 175.0 %copy-start.11 = (s32[8,4]{0,1:T(4,128)S(1)}, s32[8,4]{0,1:T(4,128)}, u32[]{:S(2)}) copy-start(s32[8,4]{0,1:T(4,128)} %param.20) | copy-start | bytes 388
  537.0 4.4 collective-permute-start.2
  542.1 200.3 %copy-start.9 = (f32[8,64]{1,0:T(8,128)S(1)}, f32[8,64]{1,0:T(8,128)}, u32[]{:S(2)}) copy-start(f32[8,64]{1,0:T(8,128)} %param.18) | copy-start | bytes 6148
  542.1 229.4 %copy-start.6 = (f32[8,4,128]{2,1,0:T(4,128)S(1)}, f32[8,4,128]{2,1,0:T(4,128)}, u32[]{:S(2)}) copy-start(f32[8,4,128]{2,1,0:T(4,128)} %param.22) | copy-start | bytes 49156
  542.1 230.8 %all-gather.25.cloned.1.call-start = ((), (), s32[]{:S(2)}) async-start(), calls=%async_computation.10 | async-start | bytes 2228224 | tf_op jit(solution)/shard_map/all_gather | solution.py:58
  646.7 3.2 collective-permute-start.3
  677.3 3.2 collective-permute-start.4
  710.0 3.2 collective-permute-start.5
  776.4 41.5 %all-to-all-start.3 = ((f32[16,1,4096]{2,1,0:T(1,128)}), f32[16,1,4096]{2,1,0:T(1,128)S(1)}, u32[]{:S(2)}, u32[]{:S(2)}) async-start(f32[16,1,4096]{2,1,0:T(1,128)} %reshape.110), calls=%async_computation.3 | async-start | bytes 524288 | tf_op jit(solution)/shard_map/all_to_all | solution.py:62
  783.0 34.0 %copy-start.13 = (f32[1024]{0:T(1024)S(1)}, f32[1024]{0:T(1024)}, u32[]{:S(2)}) copy-start(f32[1024]{0:T(1024)} %param.23) | copy-start | bytes 12292
  786.8 33.7 %copy-start.8 = (f32[8,64]{1,0:T(8,128)}, f32[8,64]{1,0:T(8,128)S(1)}, u32[]{:S(2)}) copy-start(f32[8,64]{1,0:T(8,128)S(1)} %add.75) | copy-start | bytes 6148
  (7 other events, 160.6 us)
Sparse Core Ops, SparseCore 0:
  10.7 77.5 all-gather.26
  91.1 70.0 all-gather.12
  194.1 69.3 all-gather.14
  266.4 70.1 all-gather.16
  368.2 69.3 all-gather.18
  440.4 70.1 all-gather.20
  542.3 69.3 all-gather.22
  614.5 70.5 all-gather.24
where the time goes:
time: 828 us; the launch traced here: 827 us
  waiting for transfers between devices  510 us (62%)
  blocking collectives  237 us (29%)
  matrix products  27.8 us (3%)
  starting transfers between devices  18.4 us (2%)
  between operations  15.3 us (2%)
  local copies, waits for them, and re-layouts  10.7 us (1%)
  other arithmetic  8.55 us (1%)
    all_gather x4, waiting for transfers between devices, shards(): lax.all_gather(cur_cov, 'tile', axis=0, tiled=True)  288 us
    all_gather x4, waiting for transfers between devices, shards(): lax.all_gather(product, 'tile', axis=0, tiled=True)  211 us
    unnamed x3, blocking collectives  83.4 us
    all_to_all x3, blocking collectives, shards(): lax.all_to_all(col_block, 'tile', split_axis=0, concat_axis=1, tiled=True)  65.3 us
    all_gather x1, blocking collectives, shards(): lax.all_gather(local_spread, 'tile', axis=1, tiled=True)  30.1 us
    all_gather x1, blocking collectives, shards(): lax.all_gather(cur_mean, 'tile', axis=0, tiled=True)  29.9 us
    all_gather x1, blocking collectives, shards(): lax.all_gather(local_mean, 'tile', axis=1, tiled=True)  28.3 us
  transfers between devices with their start and end apart: 15, of which 13 were waited for; matrix products, arithmetic and copies ran while one was open for 1% of the time, Pallas kernels for 0%

commit v1 on v0

--- a/solution.py
+++ b/solution.py
@@ -6,6 +6,14 @@
 TILE_STATES = 128
 SLOTS = 4
 GROUP_SEGS = 4
+
+
+def choose_rings_here(load, link_axis):
+    num = lax.axis_size(link_axis)
+    passed = range(load.ndim)
+    rack = list(map(lambda u: num if u == 0 else 1, passed))
+    earlier = jnp.tile(load, rack)
+    return lax.all_to_all(earlier, link_axis, split_axis=0, concat_axis=0, tiled=True)
 
 
 def shifted(block, axis, distance):
@@ -45,7 +53,7 @@
     for depth_step in range(GROUP_SEGS):
         whole_mean, whole_cov = (
             lax.all_gather(cur_mean, "tile", axis=0, tiled=True),
-            lax.all_gather(cur_cov, "tile", axis=0, tiled=True),
+            choose_rings_here(cur_cov, "tile"),
         )
         is_mine = slot_place == GROUP_SEGS - 1 - depth_step
         kept_mean = jnp.where(is_mine, whole_mean, kept_mean)

time: 828 us -> 975 us (1.18)
  blocking collectives: 237 us -> 651 us
  waiting for transfers between devices: 510 us -> 227 us
  local copies, waits for them, and re-layouts: 10.7 us -> 27.8 us
    all_to_all x0 -> x4, blocking collectives: none -> 412 us  [choose_rings_here(): lax.all_to_all(earlier, link_axis, split_axis=0, concat_axis=0, tiled=True)]
    all_gather x4 -> x0, waiting for transfers between devices: 288 us -> none  [shards(): lax.all_gather(cur_cov, 'tile', axis=0, tiled=True)]
  transfers between devices with their start and end apart: 15 -> 11, of which waited for: 13 -> 9; matrix products, arithmetic and copies ran while one was open for 1% -> 1% of each run, Pallas kernels for 0% -> 0%
where the time goes in v1:
time: 975 us; the launch traced here: 973 us
  blocking collectives  651 us (67%)
  waiting for transfers between devices  227 us (23%)
  local copies, waits for them, and re-layouts  27.8 us (3%)
  matrix products  22.1 us (2%)
  starting transfers between devices  17.4 us (2%)
  between operations  14.9 us (2%)
  other arithmetic  12.6 us (1%)
    all_to_all x4, blocking collectives, choose_rings_here(): lax.all_to_all(earlier, link_axis, split_axis=0, concat_axis=0, tiled=True)  412 us
    all_gather x4, waiting for transfers between devices, shards(): lax.all_gather(product, 'tile', axis=0, tiled=True)  215 us
    unnamed x3, blocking collectives  83.1 us
    all_to_all x3, blocking collectives, shards(): lax.all_to_all(col_block, 'tile', split_axis=0, concat_axis=1, tiled=True)  65.6 us
    all_gather x1, blocking collectives, shards(): lax.all_gather(cur_mean, 'tile', axis=0, tiled=True)  32 us
    all_gather x1, blocking collectives, shards(): lax.all_gather(local_spread, 'tile', axis=1, tiled=True)  30.1 us
    all_gather x1, blocking collectives, shards(): lax.all_gather(local_mean, 'tile', axis=1, tiled=True)  28.3 us
  transfers between devices with their start and end apart: 11, of which 9 were waited for; matrix products, arithmetic and copies ran while one was open for 1% of the time, Pallas kernels for 0%

profile of v1, /device:TPU:2, one launch (start us, length us, event | category | flops | bytes accessed | tf_op | source)
XLA Modules:
  0.0 973.3 jit_solution(8329140792882046638)
XLA Ops:
  8.4 111.5 %all_to_all.109 = bf16[16,64,1024]{2,1,0:T(8,128)(2,1)S(1)} all-to-all(bf16[16,64,1024]{2,1,0:T(8,128)(2,1)S(1)} %tile.11), channel_id=1, replica_groups=mesh['tm'=32,'tile'=16] {'tile'}, dimensions={0} | all-to-all | bytes 4194304 | tf_op jit(solution)/shard_map/all_to_all | solution.py:16
  121.1 68.8 %all-gather.8.cloned.1.call-done = bf16[1024,1024]{1,0:T(8,128)(2,1)} async-done(((bf16[64,1024]{1,0:T(8,128)(2,1)}), bf16[1024,1024]{1,0:T(8,128)(2,1)}) %all-gather.8.cloned.1.call-update) | async-done | bytes 2097168 | tf_op jit(solution)/shard_map/all_gather | solution.py:66
  192.5 21.7 %all_to_all.110 = f32[16,1,4096]{2,1,0:T(1,128)S(1)} all-to-all(f32[16,1,4096]{2,1,0:T(1,128)S(1)} %reshape.132), channel_id=1, replica_groups=mesh['tm'=32,'tile'=16] {'tile'}, dimensions={0} | all-to-all | bytes 524288 | tf_op jit(solution)/shard_map/all_to_all | solution.py:70
  218.7 2.5 collective-permute-done
  222.4 100.3 %all_to_all.111 = bf16[16,64,1024]{2,1,0:T(8,128)(2,1)S(1)} all-to-all(bf16[16,64,1024]{2,1,0:T(8,128)(2,1)S(1)} %tile.12), channel_id=1, replica_groups=mesh['tm'=32,'tile'=16] {'tile'}, dimensions={0} | all-to-all | bytes 4194304 | tf_op jit(solution)/shard_map/all_to_all | solution.py:16
  325.2 72.1 %all-gather.10.cloned.1.call-done = bf16[1024,1024]{1,0:T(8,128)(2,1)} async-done(((bf16[64,1024]{1,0:T(8,128)(2,1)}), bf16[1024,1024]{1,0:T(8,128)(2,1)}) %all-gather.10.cloned.1.call-update) | async-done | bytes 2097168 | tf_op jit(solution)/shard_map/all_gather | solution.py:66
  397.3 2.3 fusion.47
  400.6 21.8 %all_to_all.112 = f32[16,1,4096]{2,1,0:T(1,128)S(1)} all-to-all(f32[16,1,4096]{2,1,0:T(1,128)} %reshape.134), channel_id=1, replica_groups=mesh['tm'=32,'tile'=16] {'tile'}, dimensions={0} | all-to-all | bytes 524288 | tf_op jit(solution)/shard_map/all_to_all | solution.py:70
  430.5 2.8 collective-permute-done.1
  433.6 97.7 %all_to_all.113 = bf16[16,64,1024]{2,1,0:T(8,128)(2,1)S(1)} all-to-all(bf16[16,64,1024]{2,1,0:T(8,128)(2,1)S(1)} %tile.13), channel_id=1, replica_groups=mesh['tm'=32,'tile'=16] {'tile'}, dimensions={0} | all-to-all | bytes 4194304 | tf_op jit(solution)/shard_map/all_to_all | solution.py:16
  533.8 74.5 %all-gather.12.cloned.1.call-done = bf16[1024,1024]{1,0:T(8,128)(2,1)} async-done(((bf16[64,1024]{1,0:T(8,128)(2,1)}), bf16[1024,1024]{1,0:T(8,128)(2,1)}) %all-gather.12.cloned.1.call-update) | async-done | bytes 2097168 | tf_op jit(solution)/shard_map/all_gather | solution.py:66
  608.3 3.1 fusion.45
  613.4 22.1 %all_to_all.114 = f32[16,1,4096]{2,1,0:T(1,128)} all-to-all(f32[16,1,4096]{2,1,0:T(1,128)} %reshape.136), channel_id=1, replica_groups=mesh['tm'=32,'tile'=16] {'tile'}, dimensions={0} | all-to-all | bytes 524288 | tf_op jit(solution)/shard_map/all_to_all | solution.py:70
  635.5 2.9 reduce.2
  648.0 2.8 collective-permute-done.2
  652.0 102.9 %all_to_all.115 = bf16[16,64,1024]{2,1,0:T(8,128)(2,1)S(1)} all-to-all(bf16[16,64,1024]{2,1,0:T(8,128)(2,1)S(1)} %tile.14), channel_id=1, replica_groups=mesh['tm'=32,'tile'=16] {'tile'}, dimensions={0} | all-to-all | bytes 4194304 | tf_op jit(solution)/shard_map/all_to_all | solution.py:16
  759.6 32.0 %all-reduce = bf16[1024]{0:T(1024)(128)(2,1)S(1)} all-reduce(bf16[1024]{0:T(1024)(128)(2,1)S(1)} %dynamic-update-slice), channel_id=2, replica_groups=mesh['tm'=32,'tile'=16] {'tile'}, use_global_device_ids=true, to_apply=%add | all-reduce | flops 1024 | bytes 4096 | tf_op jit(solution)/shard_map/all_gather | solution.py:55
  795.2 27.0 %all-reduce.1 = bf16[1024]{0:T(1024)(128)(2,1)S(1)} all-reduce(bf16[1024]{0:T(1024)(128)(2,1)S(1)} %dynamic-update-slice.1), channel_id=1, replica_groups=mesh['tm'=32,'tile'=16] {'tile'}, use_global_device_ids=true, to_apply=%add.1 | all-reduce | flops 1024 | bytes 4096
  825.9 29.1 %all-reduce.2 = bf16[1024]{0:T(1024)(128)(2,1)S(1)} all-reduce(bf16[1024]{0:T(1024)(128)(2,1)S(1)} %dynamic-update-slice.2), channel_id=1, replica_groups=mesh['tm'=32,'tile'=16] {'tile'}, use_global_device_ids=true, to_apply=%add.2 | all-reduce | flops 1024 | bytes 4096
  858.5 27.0 %all-reduce.3 = bf16[1024]{0:T(1024)(128)(2,1)S(1)} all-reduce(bf16[1024]{0:T(1024)(128)(2,1)S(1)} %dynamic-update-slice.3), channel_id=1, replica_groups=mesh['tm'=32,'tile'=16] {'tile'}, use_global_device_ids=true, to_apply=%add.3 | all-reduce | flops 1024 | bytes 4096
  887.3 28.3 %all-gather.1 = f32[16,64,8]{1,2,0:T(8,128)S(1)} all-gather(f32[1,64,8]{1,2,0:T(8,128)S(1)} %bitcast.168), channel_id=1, replica_groups=mesh['tm'=32,'tile'=16] {'tile'}, dimensions={0}, use_global_device_ids=true | all-gather | bytes 34816 | tf_op jit(solution)/shard_map/all_gather | solution.py:91
  923.6 5.5 all-to-all-start.7
  929.2 3.8 fusion
  933.0 30.1 %all-gather.2 = f32[16,64,8]{1,2,0:T(8,128)S(1)} all-gather(f32[1,64,8]{1,2,0:T(8,128)S(1)} %bitcast.169), channel_id=1, replica_groups=mesh['tm'=32,'tile'=16] {'tile'}, dimensions={0}, use_global_device_ids=true | all-gather | bytes 34816 | tf_op jit(solution)/shard_map/all_gather | solution.py:92
  (134 shorter events, 65.9 us)
Async XLA Ops:
  7.2 112.8 %copy-start = (bf16[1,64,1024]{2,1,0:T(8,128)(2,1)S(1)}, bf16[1,64,1024]{2,1,0:T(8,128)(2,1)}, u32[]{:S(2)}) copy-start(bf16[1,64,1024]{2,1,0:T(8,128)(2,1)} %param.12) | copy-start | bytes 393220
  7.2 182.7 %all-gather.8.cloned.1.call-start = ((), (), s32[]{:S(2)}) async-start(), calls=%async_computation.8 | async-start | bytes 2228224 | tf_op jit(solution)/shard_map/all_gather | solution.py:66
  121.1 276.2 %all-gather.10.cloned.1.call-start = ((), (), s32[]{:S(2)}) async-start(), calls=%async_computation.9 | async-start | bytes 2228224 | tf_op jit(solution)/shard_map/all_gather | solution.py:66
  216.8 4.4 collective-permute-start
  325.2 283.1 %all-gather.12.cloned.1.call-start = ((), (), s32[]{:S(2)}) async-start(), calls=%async_computation.10 | async-start | bytes 2228224 | tf_op jit(solution)/shard_map/all_gather | solution.py:66
  428.6 4.7 collective-permute-start.1
  433.3 97.9 %copy-start.5 = (bf16[64,1024]{1,0:T(8,128)(2,1)}, bf16[64,1024]{1,0:T(8,128)(2,1)S(1)}, u32[]{:S(2)}) copy-start(bf16[64,1024]{1,0:T(8,128)(2,1)S(1)} %broadcast_select_fusion.1) | copy-start | bytes 393220
  533.7 386.5 %all-gather.14.cloned.1.call-start = ((), (), s32[]{:S(2)}) async-start(), calls=%async_computation.11 | async-start | bytes 2228224 | tf_op jit(solution)/shard_map/all_gather | solution.py:66
  613.4 37.4 %copy-start.6 = (bf16[64,1024]{1,0:T(8,128)(2,1)S(1)}, bf16[64,1024]{1,0:T(8,128)(2,1)}, u32[]{:S(2)}) copy-start(bf16[64,1024]{1,0:T(8,128)(2,1)} %copy-done.5) | copy-start | bytes 393220
  646.1 4.7 collective-permute-start.2
  754.9 36.8 %copy-start.19 = (f32[1,64]{1,0:T(1,128)S(1)}, f32[1,64]{1,0:T(1,128)}, u32[]{:S(2)}) copy-start(f32[1,64]{1,0:T(1,128)} %param.13) | copy-start | bytes 772
  754.9 69.5 %copy-start.18 = (s32[8]{0:T(128)S(1)}, s32[8]{0:T(128)}, u32[]{:S(2)}) copy-start(s32[8]{0:T(128)} %param.21) | copy-start | bytes 100
  754.9 102.1 %copy-start.15 = (s32[8,4]{0,1:T(4,128)S(1)}, s32[8,4]{0,1:T(4,128)}, u32[]{:S(2)}) copy-start(s32[8,4]{0,1:T(4,128)} %param.20) | copy-start | bytes 388
  754.9 132.4 %copy-start.13 = (f32[8,64]{1,0:T(8,128)S(1)}, f32[8,64]{1,0:T(8,128)}, u32[]{:S(2)}) copy-start(f32[8,64]{1,0:T(8,128)} %param.18) | copy-start | bytes 6148
  756.2 160.1 %copy-start.10 = (f32[8,4,128]{2,1,0:T(4,128)S(1)}, f32[8,4,128]{2,1,0:T(4,128)}, u32[]{:S(2)}) copy-start(f32[8,4,128]{2,1,0:T(4,128)} %param.22) | copy-start | bytes 49156
  791.8 3.2 collective-permute-start.3
  822.4 3.2 collective-permute-start.4
  855.1 3.2 collective-permute-start.5
  887.3 35.2 %copy-start.11 = (f32[8,64]{1,0:T(8,128)}, f32[8,64]{1,0:T(8,128)S(1)}, u32[]{:S(2)}) copy-start(f32[8,64]{1,0:T(8,128)S(1)} %add.74) | copy-start | bytes 6148
  923.6 40.4 %all-to-all-start.7 = ((f32[16,1,4096]{2,1,0:T(1,128)}), f32[16,1,4096]{2,1,0:T(1,128)S(1)}, u32[]{:S(2)}, u32[]{:S(2)}) async-start(f32[16,1,4096]{2,1,0:T(1,128)} %reshape.138), calls=%async_computation.7 | async-start | bytes 524288 | tf_op jit(solution)/shard_map/all_to_all | solution.py:70
  929.2 34.0 %copy-start.17 = (f32[1024]{0:T(1024)S(1)}, f32[1024]{0:T(1024)}, u32[]{:S(2)}) copy-start(f32[1024]{0:T(1024)} %param.23) | copy-start | bytes 12292
  932.9 33.1 %copy-start.7 = (f32[1,64,1024]{2,1,0:T(8,128)S(1)}, f32[1,64,1024]{2,1,0:T(8,128)}, u32[]{:S(2)}) copy-start(f32[1,64,1024]{2,1,0:T(8,128)} %all_to_all.100) | copy-start | bytes 786436
  933.0 33.1 %copy-start.8 = (f32[1,64,1024]{2,1,0:T(8,128)S(1)}, f32[1,64,1024]{2,1,0:T(8,128)}, u32[]{:S(2)}) copy-start(f32[1,64,1024]{2,1,0:T(8,128)} %all_to_all.99) | copy-start | bytes 786436
  933.0 33.8 %copy-start.12 = (f32[8,64]{1,0:T(8,128)}, f32[8,64]{1,0:T(8,128)S(1)}, u32[]{:S(2)}) copy-start(f32[8,64]{1,0:T(8,128)S(1)} %add.75) | copy-start | bytes 6148
  (7 other events, 69.8 us)
Sparse Core Ops, SparseCore 0:
  121.2 68.6 all-gather.7
  325.3 71.9 all-gather.9
  533.9 74.3 all-gather.11
  757.5 69.1 all-gather.13
